TPU v7x, 32 devices: a whole 2x2x4 slice. The times are simulated.
32 devices in a mesh: ta: 8 (over z, x), ba: 4 (over y, core).
Axes of the slice: x: 2, y: 2, z: 4, core: 2. Of those that a mesh axis runs over, the one named last changes fastest.
Arguments:
- samples: int32 [262144, 512], P('ta', 'ba'), may hold values from -128 to 127
- input_gain: float32 [512], P('ba'), may hold values from 0.005 to 0.03
- pfb_weights: float32 [16, 1024], replicated, may hold values from -1.5 to 1.5
- chan_map: int32 [512], replicated, may hold values from 0 to 511, each once
Outputs:
- visibility: float32 [2, 512, 512, 512], P(None, ('ta', 'ba'))
Inputs may be any that keep to these rules, and one draw needn't show every extreme that they name: `chan_map`: each of the 512 channel numbers appears exactly once.
All inputs are finite; a program needn't handle non-finite values.
Results may differ from a plain program's by a relative error of at most 0.0036.
Values may be sent and summed in bfloat16 or wider, within the bound.
A program may use at most 192 MiB of HBM per device.

v0:
```python
import math

import jax
import jax.numpy as jnp
from jax import lax
from jax.sharding import PartitionSpec as P


def from_behind(block, axis, distance):
    devices = range(lax.axis_size(axis))
    route = [(i - distance, i) for i in devices if i - distance in devices]
    return lax.ppermute(block, axis, route)


def build_table(chan_map, frame_len):
    sample_idx = jnp.arange(frame_len, dtype=jnp.int32)
    product = sample_idx[:, None] * chan_map[None, :] % frame_len
    angle = product.astype(jnp.float32) * (2.0 * math.pi / frame_len)
    scale = 1.0 / math.sqrt(frame_len)
    stacked = jnp.stack([jnp.cos(angle) * scale, -jnp.sin(angle) * scale], axis=-1)
    return stacked.reshape(frame_len, -1).astype(jnp.bfloat16)


def rotate_pair(values):
    return jnp.stack([values[..., 1], -values[..., 0]], axis=-1)


def per_device(samples, input_gain, pfb_weights, chan_map):
    tap_count = pfb_weights.shape[0]
    frame_len = pfb_weights.shape[1]
    row_count, inputs_dev = samples.shape
    spectra_dev = row_count // frame_len
    calibrated = (samples.astype(jnp.float32) * input_gain[None, :]).astype(jnp.bfloat16)
    frames = calibrated.reshape(spectra_dev, frame_len, inputs_dev)
    history = from_behind(frames[spectra_dev - (tap_count - 1) :], "ta", 1)
    weights = pfb_weights[:, :, None]
    extended = jnp.concatenate([history, frames], axis=0)
    running = jnp.zeros((spectra_dev, frame_len, inputs_dev), jnp.float32)
    for tap_index in range(tap_count):
        running = running + weights[tap_index] * extended[
            tap_index : tap_index + spectra_dev
        ].astype(jnp.float32)
    filtered = running.astype(jnp.bfloat16)
    dft_table = build_table(chan_map, frame_len)
    spectra = jnp.einsum(
        "sni,nk->sik", filtered, dft_table, preferred_element_type=jnp.float32
    ).astype(jnp.bfloat16)
    turned = lax.all_to_all(
        lax.all_to_all(spectra, "ta", split_axis=2, concat_axis=0, tiled=True),
        "ba",
        split_axis=2,
        concat_axis=1,
        tiled=True,
    )
    total_spectra = turned.shape[0]
    cells = turned.reshape(total_spectra, turned.shape[1], turned.shape[2] // 2, 2)
    stacked = jnp.stack([cells, rotate_pair(cells)], axis=0)
    products = jnp.einsum("osicp,sjcp->ocij", stacked, cells, preferred_element_type=jnp.float32)
    return products / total_spectra


def solution(mesh):
    placed = (P("ta", "ba"), P("ba"), P(), P())
    return jax.shard_map(
        per_device,
        mesh=mesh,
        in_specs=placed,
        out_specs=P(None, ("ta", "ba"), None, None),
        check_vma=False,
    )
```

profile of v0, /device:TPU:15, one launch (start us, length us, event | category | flops | bytes accessed | tf_op | source)
XLA Modules:
  0.0 586.8 jit_solution(13740697735559772385)
XLA Ops:
  0.0 6.8 %multiply_convert_fusion = bf16[32768,128]{1,0:T(8,128)(2,1)S(1)} fusion(s32[32768,128]{1,0:T(8,128)} %param.4, f32[128]{0:T(128)} %param.5), kind=kLoop, calls=%fused_computation.35 | loop fusion | flops 12582912 | bytes 25166336 | tf_op jit(solution)/shard_map/convert_element_type | solution.py:33
  6.8 0.0 copy-start
  6.8 3.4 copy-done
  10.2 0.0 copy-start.2
  10.2 2.0 slice.156
  12.2 6.2 %copy.44 = bf16[15,1024,128]{1,2,0:T(8,128)(2,1)} copy(bf16[15,1024,128]{2,1,0:T(8,128)(2,1)} %bitcast.55) | data formatting | bytes 7864320 | tf_op jit(solution)/shard_map/slice | solution.py:35
  18.4 3.2 collective-permute-start
  21.6 0.0 copy-done.2
  21.6 8.7 %multiply_convert_fusion.2 = (bf16[1024,512,1]{1,0,2:T(8,128)(2,1)S(1)}, bf16[1024,512,1]{1,0,2:T(8,128)(2,1)S(1)}) fusion(s32[512]{0:T(512)S(1)} %copy-done.2), kind=kLoop, calls=%fused_computation.65 | loop fusion | flops 9961472 | bytes 2099200 | tf_op jit(solution)/shard_map/convert
  30.3 0.2 pad_maximum_fusion.1
  30.5 4.0 copy.47
  34.5 2.7 convert_element_type.98
  37.2 0.0 copy-start.1
  37.3 12.0 %copy.45 = bf16[32,1024,128]{1,2,0:T(8,128)(2,1)} copy(bf16[32,1024,128]{2,1,0:T(8,128)(2,1)} %bitcast.51) | data formatting | bytes 16777216 | tf_op jit(solution)/shard_map/reshape | solution.py:34
  49.3 0.0 copy-done.1
  49.3 57.1 %collective-permute-done = bf16[15,1024,128]{1,2,0:T(8,128)(2,1)} collective-permute-done((bf16[15,1024,128]{1,2,0:T(8,128)(2,1)}, bf16[15,1024,128]{1,2,0:T(8,128)(2,1)}, u32[]{:S(2)}, u32[]{:S(2)}) %collective-permute-start) | collective-permute-done | bytes 3932192 | tf_op jit(solution)/shard_map/ppermute | solution.py:12
  106.4 57.1 %fusion.23 = bf16[32,128,1024]{2,1,0:T(8,128)(2,1)} fusion(bf16[32,1024,128]{1,2,0:T(8,128)(2,1)} %copy.45, bf16[15,1024,128]{1,2,0:T(8,128)(2,1)} %collective-permute-done, f32[1024]{0:T(1024)S(1)} %bitcast.70, f32[1024]{0:T(1024)S(1)} %bitcast.71, f32[1024]{0:T(1024)S(1)} %bitcast.57, f32[1024]{0:T(1024)S(1)} %bitcast.58, f32[1024]{0:T(1024)S(1)} %bitcast.59, ...), kind=kOutput, calls=%fused_computation.54 | convolution fusion | flops 8858370048 | bytes 22872064 | tf_op jit(solution)/shard_map/sni,nk->sik/dot_general | solution.py:45
  163.5 12.5 %copy.49 = bf16[32,128,1024]{1,0,2:T(8,128)(2,1)} copy(bf16[32,128,1024]{2,1,0:T(8,128)(2,1)} %fusion.23) | data formatting | bytes 16777216 | tf_op jit(solution)/shard_map/convert_element_type | solution.py:47
  176.0 185.9 %all_to_all.33 = bf16[32,128,1024]{1,0,2:T(8,128)(2,1)} all-to-all(bf16[32,128,1024]{1,0,2:T(8,128)(2,1)} %copy.49), channel_id=1, replica_groups=mesh['ta'=8,'ba'=4] {'ta'}, dimensions={2} | all-to-all | bytes 16777216 | tf_op jit(solution)/shard_map/all_to_all | solution.py:49
  361.9 12.7 %copy.51 = bf16[8,32,128,128]{3,2,1,0:T(8,128)(2,1)} copy(bf16[8,32,128,128]{2,1,3,0:T(8,128)(2,1)} %bitcast.52) | data formatting | bytes 16777216 | tf_op jit(solution)/shard_map/all_to_all | solution.py:49
  374.6 11.9 %copy.52 = bf16[256,128,128]{1,0,2:T(8,128)(2,1)} copy(bf16[256,128,128]{2,1,0:T(8,128)(2,1)} %bitcast.53) | data formatting | bytes 16777216 | tf_op jit(solution)/shard_map/all_to_all | solution.py:49
  386.5 98.3 %all_to_all.34 = bf16[256,128,128]{1,0,2:T(8,128)(2,1)S(1)} all-to-all(bf16[256,128,128]{1,0,2:T(8,128)(2,1)} %copy.52), channel_id=1, replica_groups=mesh['ta'=8,'ba'=4] {'ba'}, dimensions={2} | all-to-all | bytes 16777216 | tf_op jit(solution)/shard_map/all_to_all | solution.py:48
  484.8 7.5 %copy.54 = bf16[256,4,128,32]{2,1,0,3:T(4,128)(2,1)} copy(bf16[256,4,128,32]{2,0,3,1:T(8,128)(2,1)S(1)} %bitcast.54) | data formatting | bytes 16777216 | tf_op jit(solution)/shard_map/all_to_all | solution.py:48
  492.3 13.1 %reshape.147 = bf16[256,512,16,2]{1,0,3,2:T(8,128)(2,1)} reshape(bf16[256,4,128,32]{2,1,0,3:T(4,128)(2,1)} %copy.54) | data formatting | bytes 16777216 | tf_op jit(solution)/shard_map/reshape | solution.py:56
  505.4 13.1 %stack_reshape.3 = bf16[1,256,512,16,2]{2,1,4,0,3:T(8,128)(2,1)} reshape(bf16[256,4,128,32]{2,1,0,3:T(4,128)(2,1)} %copy.54) | data formatting | bytes 16777216 | tf_op jit(solution)/shard_map/stack;reshape | solution.py:57
  518.4 5.1 fusion.33
  523.5 6.4 %maximum_bitcast_fusion = bf16[1,256,512,16,2]{2,1,4,0,3:T(8,128)(2,1)} fusion(bf16[256,512,16,1]{1,0,3,2:T(8,128)(2,1)} %get-tuple-element.6, bf16[256,512,16,1]{1,0,3,2:T(8,128)(2,1)S(1)} %get-tuple-element.5), kind=kLoop, calls=%fused_computation.51 | loop fusion | flops 4194304 | bytes 16777216 | tf_op jit(solution)/shard_map/stack | solution.py:57
  529.9 23.0 %fusion = f32[2,16,512,512]{2,3,0,1:T(8,128)} fusion(bf16[1,256,512,16,2]{2,1,4,0,3:T(8,128)(2,1)} %maximum_bitcast_fusion, bf16[1,256,512,16,2]{2,1,4,0,3:T(8,128)(2,1)} %stack_reshape.3, bf16[256,512,16,2]{1,0,3,2:T(8,128)(2,1)} %reshape.147), kind=kOutput, calls=%fused_computation.15 | convolution fusion | flops 8631877632 | bytes 58720256 | tf_op jit(solution)/shard_map/osicp,sjcp->ocij/dot_general | solution.py:58
  552.8 34.0 %copy.57 = f32[2,16,512,512]{3,2,1,0:T(8,128)} copy(f32[2,16,512,512]{2,3,0,1:T(8,128)} %fusion) | data formatting | bytes 67108864 | tf_op jit(solution)/shard_map/div | solution.py:59
  (1 shorter events, 0.0 us)
Async XLA Ops:
  6.8 3.4 copy-start
  10.2 11.4 %copy-start.2 = (s32[512]{0:T(512)S(1)}, s32[512]{0:T(512)}, u32[]{:S(2)}) copy-start(s32[512]{0:T(512)} %param.7) | copy-start | bytes 6148
  18.4 88.0 %collective-permute-start = (bf16[15,1024,128]{1,2,0:T(8,128)(2,1)}, bf16[15,1024,128]{1,2,0:T(8,128)(2,1)}, u32[]{:S(2)}, u32[]{:S(2)}) collective-permute-start(bf16[15,1024,128]{1,2,0:T(8,128)(2,1)} %copy.44), channel_id=1, source_target_pairs={{0,4},{4,8},{8,12},{12,16},{16,20},{20,24},{24,28},{1,5},{5,9},{9,... | collective-permute-start | bytes 11796488 | tf_op jit(solution)/shard_map/ppermute | solution.py:12
  37.2 12.0 %copy-start.1 = (f32[16,1024]{1,0:T(8,128)S(1)}, f32[16,1024]{1,0:T(8,128)}, u32[]{:S(2)}) copy-start(f32[16,1024]{1,0:T(8,128)} %param.6) | copy-start | bytes 196612
where the time goes:
time: 594 us; the launch traced here: 587 us
  blocking collectives  284 us (48%)
  local copies, waits for them, and re-layouts  135 us (23%)
  matrix products  80.1 us (13%)
  waiting for transfers between devices  57.1 us (10%)
  other arithmetic  27.1 us (5%)
    all_to_all x1, blocking collectives, per_device(): lax.all_to_all(spectra, 'ta', split_axis=2, concat_axis=0, tiled=True)  186 us
    all_to_all x1, blocking collectives, per_device(): lax.all_to_all(lax.all_to_all(spectra, 'ta', split_axis=2, concat_axis=0,...  98.3 us
    ppermute x1, waiting for transfers between devices, from_behind(): return lax.ppermute(block, axis, route)  57.1 us
    dot_general x1, matrix products, per_device(): jnp.einsum('sni,nk->sik', filtered, dft_table, preferred_element_type=jnp...  57.1 us
    div x1, local copies, waits for them, and re-layouts, per_device(): return products / total_spectra  34 us
    all_to_all x2, local copies, waits for them, and re-layouts, per_device(): lax.all_to_all(spectra, 'ta', split_axis=2, concat_axis=0, tiled=True)  24.6 us
    dot_general x1, matrix products, per_device(): jnp.einsum('osicp,sjcp->ocij', stacked, cells, preferred_element_type=jnp...  23 us
    reshape x1, local copies, waits for them, and re-layouts, per_device(): turned.reshape(total_spectra, turned.shape[1], turned.shape[2] // 2, 2)  13.1 us
  transfers between devices with their start and end apart: 1, of which 1 were waited for; matrix products, arithmetic and copies ran while one was open for 5% of the time, Pallas kernels for 0%

commit v1 on v0

v1 whole, which is shorter than its diff:
```python
import functools
import math

import jax
import jax.numpy as jnp
from jax import lax
from jax.experimental import pallas as pl
from jax.experimental.pallas import tpu as pltpu
from jax.sharding import PartitionSpec as P

MESH = pl.DeviceIdType.MESH
CHUNK = 16
ROWS = 256


def table_factors(chan_map, frame_len):
    chan = jnp.repeat(chan_map, 2)
    quarter = jnp.tile(jnp.array([0, frame_len // 4], jnp.int32), chan_map.shape[0])
    step = 2.0 * math.pi / frame_len
    blocks = jnp.arange(frame_len // 128, dtype=jnp.int32) * 128
    lanes = jnp.arange(128, dtype=jnp.int32)
    coarse = ((chan[:, None] * blocks[None, :] + quarter[:, None]) % frame_len).astype(jnp.float32) * step
    fine = (chan[:, None] * lanes[None, :] % frame_len).astype(jnp.float32) * step
    scale = 1.0 / math.sqrt(frame_len)
    coarse_pair = jnp.concatenate([jnp.cos(coarse) * scale, jnp.sin(coarse) * scale], axis=1)
    return coarse_pair, jnp.cos(fine), jnp.sin(fine)


def turn_kernel(
    shape, samples, gain, weights, coarse, fine_cos, fine_sin, received,
    raw, cal, filtered, table, partial, spectra,
    load_sem, halo_send, halo_recv, send_sem, recv_sem, own_sem,
):
    n_ta, n_ba, taps, frames, frame_len = shape
    n_dev = n_ta * n_ba
    halo = taps - 1
    ta, ba = lax.axis_index("ta"), lax.axis_index("ba")
    me = ta * n_ba + ba
    table_rows = table.shape[0]
    rows_dev = table_rows // n_dev
    blocks = table_rows // ROWS
    dests = n_dev // blocks

    late = pltpu.make_async_copy(samples.at[pl.ds(frames - halo, halo)], raw.at[pl.ds(frames - halo, halo)], load_sem.at[0])
    early = pltpu.make_async_copy(samples.at[pl.ds(0, frames - halo)], raw.at[pl.ds(0, frames - halo)], load_sem.at[1])
    late.start()
    early.start()

    barrier = pltpu.get_barrier_semaphore()

    @pl.loop(1, n_dev)
    def _(step):
        other = lax.rem(me + step, n_dev)
        pl.semaphore_signal(
            barrier, inc=1, device_id=(other // n_ba, lax.rem(other, n_ba)), device_id_type=MESH
        )

    def calibrate(first, count):
        pieces = frame_len // 128

        @pl.loop(0, count * pieces)
        def _(step):
            frame = first + step // pieces
            rows = pl.ds(pl.multiple_of(lax.rem(step, pieces) * 128, 128), 128)
            value = raw[frame, rows, :].astype(jnp.float32) * gain[...]
            cal[frame + halo, rows, :] = value.astype(jnp.bfloat16)

    late.wait()
    calibrate(frames - halo, halo)
    pl.semaphore_wait(barrier, n_dev - 1)

    halo_copy = pltpu.make_async_remote_copy(
        src_ref=cal.at[pl.ds(frames, halo)],
        dst_ref=cal.at[pl.ds(0, halo)],
        send_sem=halo_send,
        recv_sem=halo_recv,
        device_id=(jnp.minimum(ta + 1, n_ta - 1), ba),
        device_id_type=MESH,
    )

    @pl.when(ta < n_ta - 1)
    def _():
        halo_copy.start()

    for a in range(frame_len // 128):
        cos_a = coarse[:, a : a + 1]
        sin_a = coarse[:, a + frame_len // 128 : a + frame_len // 128 + 1]
        table[:, a * 128 : (a + 1) * 128] = (fine_cos[...] * cos_a - fine_sin[...] * sin_a).astype(jnp.bfloat16)

    early.wait()
    calibrate(0, frames - halo)

    lower = 1 - ta // (n_ta // 2)

    def message(q, dest):
        return pltpu.make_async_remote_copy(
            src_ref=spectra.at[q, pl.ds(dest * rows_dev, rows_dev)],
            dst_ref=received.at[q, me],
            send_sem=send_sem.at[q, dest],
            recv_sem=recv_sem.at[q, me],
            device_id=(dest // n_ba, lax.rem(dest, n_ba)),
            device_id_type=MESH,
        )

    def own(q):
        return pltpu.make_async_copy(
            spectra.at[q, pl.ds(me * rows_dev, rows_dev)], received.at[q, me], own_sem.at[q]
        )

    n_chunks = frames // CHUNK

    @pl.loop(0, n_chunks)
    def _(chunk):
        q = n_chunks - 1 - chunk

        @pl.when(jnp.logical_and(chunk == n_chunks - 1, ta > 0))
        def _():
            halo_copy.wait_recv()

        @pl.when(jnp.logical_and(chunk == n_chunks - 1, ta == 0))
        def _():
            @pl.loop(0, halo)
            def _(frame):
                cal[frame] = jnp.zeros((frame_len, 128), jnp.bfloat16)

        @pl.loop(0, frame_len // 16)
        def _(block):
            rows = pl.ds(pl.multiple_of(block * 16, 16), 16)
            own_weights = weights[rows, :]
            taps_here = [jnp.broadcast_to(own_weights[:, t : t + 1], (16, 128)) for t in range(taps)]
            for group in range(CHUNK // 4):
                sums = [None] * 4
                for f in range(taps + 3):
                    x = cal[q * CHUNK + group * 4 + f, rows, :].astype(jnp.float32)
                    for j in range(4):
                        t = f - j
                        if 0 <= t < taps:
                            term = taps_here[t] * x
                            sums[j] = term if sums[j] is None else sums[j] + term
                for j in range(4):
                    s = group * 4 + j
                    filtered[s // 2, rows, (s % 2) * 128 : (s % 2 + 1) * 128] = sums[j].astype(jnp.bfloat16)

        @pl.loop(0, blocks)
        def _(p):
            b = p + (blocks - 1 - 2 * p) * lower
            base = pl.multiple_of(b * ROWS, ROWS)
            left = table[pl.ds(base, ROWS), :]

            @pl.loop(0, CHUNK // 2)
            def _(pair):
                result = jnp.dot(left, filtered[pair], preferred_element_type=jnp.float32)
                start = pl.multiple_of(pair * 2 * ROWS, ROWS)
                partial[pl.ds(start, ROWS), :] = result[:, :128]
                partial[pl.ds(start + ROWS, ROWS), :] = result[:, 128:]

            @pl.loop(0, ROWS // 8)
            def _(k8):
                for r in range(8):
                    k = k8 * 8 + r
                    spectra[q, base + k] = partial[pl.ds(k, CHUNK, stride=ROWS), :].astype(jnp.bfloat16)

            @pl.loop(0, dests)
            def _(j):
                dest = b * dests + lax.rem(j + me, dests)

                @pl.when(dest != me)
                def _():
                    message(q, dest).start()

                @pl.when(dest == me)
                def _():
                    own(q).start()

    @pl.when(ta < n_ta - 1)
    def _():
        halo_copy.wait_send()

    @pl.loop(0, n_chunks)
    def _(q):
        own(q).wait()

        @pl.loop(1, n_dev)
        def _(step):
            other = lax.rem(me + step, n_dev)
            message(q, other).wait_send()
            pltpu.make_async_remote_copy(
                src_ref=spectra.at[q, pl.ds(other * rows_dev, rows_dev)],
                dst_ref=received.at[q, other],
                send_sem=send_sem.at[q, other],
                recv_sem=recv_sem.at[q, other],
                device_id=(other // n_ba, lax.rem(other, n_ba)),
                device_id_type=MESH,
            ).wait_recv()


def correlate_kernel(scale, received, out):
    n_chunks, n_ta, n_ba = received.shape[:3]
    depth = n_chunks * n_ta * received.shape[4]

    def part(p):
        return jnp.concatenate(
            [received[:, :, b, p].reshape(depth, 128) for b in range(n_ba)], axis=1
        )

    re, im = part(0), part(1)
    right = jnp.concatenate([re, im], axis=0)
    re_t, im_t = re.T, im.T
    out[0, 0] = jnp.dot(jnp.concatenate([re_t, im_t], axis=1), right, preferred_element_type=jnp.float32) * scale
    out[1, 0] = jnp.dot(jnp.concatenate([im_t, -re_t], axis=1), right, preferred_element_type=jnp.float32) * scale


def per_device(samples, input_gain, pfb_weights, chan_map):
    taps, frame_len = pfb_weights.shape
    frames = samples.shape[0] // frame_len
    n_ta, n_ba = lax.axis_size("ta"), lax.axis_size("ba")
    n_dev = n_ta * n_ba
    table_rows = 2 * chan_map.shape[0]
    rows_dev = table_rows // n_dev
    n_chunks = frames // CHUNK
    inputs = n_ba * samples.shape[1]
    coarse, fine_cos, fine_sin = table_factors(chan_map, frame_len)
    vmem = pl.BlockSpec(memory_space=pltpu.VMEM)
    hbm = pl.BlockSpec(memory_space=pl.ANY)
    received = pl.pallas_call(
        functools.partial(turn_kernel, (n_ta, n_ba, taps, frames, frame_len)),
        out_shape=jax.ShapeDtypeStruct((n_chunks, n_dev, rows_dev, CHUNK, 128), jnp.bfloat16),
        in_specs=[hbm, vmem, vmem, vmem, vmem, vmem],
        out_specs=hbm,
        scratch_shapes=[
            pltpu.VMEM((frames, frame_len, 128), jnp.int32),
            pltpu.VMEM((frames + taps - 1, frame_len, 128), jnp.bfloat16),
            pltpu.VMEM((CHUNK // 2, frame_len, 256), jnp.bfloat16),
            pltpu.VMEM((table_rows, frame_len), jnp.bfloat16),
            pltpu.VMEM((CHUNK * ROWS, 128), jnp.float32),
            pltpu.VMEM((n_chunks, table_rows, CHUNK, 128), jnp.bfloat16),
            pltpu.SemaphoreType.DMA((2,)),
            pltpu.SemaphoreType.DMA,
            pltpu.SemaphoreType.DMA,
            pltpu.SemaphoreType.DMA((n_chunks, n_dev)),
            pltpu.SemaphoreType.DMA((n_chunks, n_dev)),
            pltpu.SemaphoreType.DMA((n_chunks,)),
        ],
        compiler_params=pltpu.CompilerParams(
            collective_id=0, has_side_effects=True, vmem_limit_bytes=56 * 1024 * 1024
        ),
        name="filter_turn",
    )(samples.reshape(frames, frame_len, 128), input_gain[None, :], pfb_weights.T, coarse, fine_cos, fine_sin)
    received = received.reshape(n_chunks, n_ta, n_ba, rows_dev, CHUNK, 128)
    channels_dev = rows_dev // 2
    return pl.pallas_call(
        functools.partial(correlate_kernel, 1.0 / (n_ta * frames)),
        grid=(channels_dev,),
        out_shape=jax.ShapeDtypeStruct((2, channels_dev, inputs, inputs), jnp.float32),
        in_specs=[pl.BlockSpec((n_chunks, n_ta, n_ba, 2, CHUNK, 128), lambda c: (0, 0, 0, c, 0, 0))],
        out_specs=pl.BlockSpec((2, 1, inputs, inputs), lambda c: (0, c, 0, 0)),
        compiler_params=pltpu.CompilerParams(vmem_limit_bytes=48 * 1024 * 1024),
        name="correlate",
    )(received)


def solution(mesh):
    placed = (P("ta", "ba"), P("ba"), P(), P())
    return jax.shard_map(
        per_device,
        mesh=mesh,
        in_specs=placed,
        out_specs=P(None, ("ta", "ba"), None, None),
        check_vma=False,
    )
```

time: 594 us -> 316 us (0.53)
  Pallas kernels: 0 us -> 305 us
  blocking collectives: 284 us -> 0 us
  local copies, waits for them, and re-layouts: 135 us -> 4.05 us
  matrix products: 80.1 us -> 0 us
  waiting for transfers between devices: 57.1 us -> 0 us
  other arithmetic: 27.1 us -> 3.45 us
    pallas_call x0 -> x2, Pallas kernels: none -> 305 us  [the longest x1 285 us: per_device(): pl.pallas_call(functools.partial(turn_kernel, (n_ta, n_ba, taps, frames,...]
    all_to_all x2 -> x0, blocking collectives: 284 us -> none  [the longest x1 186 us: per_device(): lax.all_to_all(spectra, 'ta', split_axis=2, concat_axis=0, tiled=True)]
    dot_general x2 -> x0, matrix products: 80.1 us -> none  [the longest x1 57.1 us: per_device(): jnp.einsum('sni,nk->sik', filtered, dft_table, preferred_element_type=jnp...]
    ppermute x1 -> x0, waiting for transfers between devices: 57.1 us -> none  [from_behind(): return lax.ppermute(block, axis, route)]
    div x1 -> x0, local copies, waits for them, and re-layouts: 34 us -> none  [per_device(): return products / total_spectra]
    all_to_all x3 -> x0, local copies, waits for them, and re-layouts: 32 us -> none  [the longest x2 24.6 us: per_device(): lax.all_to_all(spectra, 'ta', split_axis=2, concat_axis=0, tiled=True)]
    reshape x2 -> x0, local copies, waits for them, and re-layouts: 25.1 us -> none  [the longest x1 13.1 us: per_device(): turned.reshape(total_spectra, turned.shape[1], turned.shape[2] // 2, 2)]
    another operation x2 -> x1, local copies, waits for them, and re-layouts: 17.1 us -> 0.02 us  [table_factors(): jnp.tile(jnp.array([0, frame_len // 4], jnp.int32), chan_map.shape[0])]
  transfers between devices with their start and end apart: 1 -> 0, of which waited for: 1 -> 0; matrix products, arithmetic and copies ran while one was open for 5% -> 0% of each run, Pallas kernels for 0% -> 0%
where the time goes in v1:
time: 316 us; the launch traced here: 313 us
  Pallas kernels  305 us (97%)
  local copies, waits for them, and re-layouts  4.05 us (1%)
  other arithmetic  3.45 us (1%)
    pallas_call x1, Pallas kernels, per_device(): pl.pallas_call(functools.partial(turn_kernel, (n_ta, n_ba, taps, frames,...  285 us
    pallas_call x1, Pallas kernels, per_device(): pl.pallas_call(functools.partial(correlate_kernel, 1.0 / (n_ta * frames))...  20.7 us

profile of v1, /device:TPU:15, one launch (start us, length us, event | category | flops | bytes accessed | tf_op | source)
XLA Modules:
  0.0 312.9 jit_solution(16150476779571893870)
XLA Ops:
  0.0 0.2 add.22
  0.2 0.8 broadcast_in_dim.9
  1.0 0.2 mul.53
  1.2 0.2 cosine_multiply_fusion
  1.4 1.1 copy.9.coarse
  2.5 1.8 copy.8
  4.3 3.2 %fusion.6 = (f32[1024,128]{1,0:T(8,128)}, f32[1024,128]{1,0:T(8,128)}) fusion(s32[1024]{0:T(1024)S(1)} %mul.53), kind=kLoop, calls=%fused_computation.9 | loop fusion | flops 1835008 | bytes 1052672 | tf_op jit(solution)/shard_map/sin | solution.py:26
  7.5 284.6 %filter_turn.1 = bf16[2,32,32,16,128]{4,3,2,1,0:T(8,128)(2,1)} custom-call(s32[32,1024,128]{2,1,0:T(8,128)} %bitcast.5, f32[1,128]{1,0:T(1,128)} %bitcast.7, f32[1024,16]{1,0:T(8,128)} %bitcast.6, f32[1024,16]{1,0:T(8,128)} %copy.9.coarse, f32[1024,128]{1,0:T(8,128)} %get-tuple-element.8.fine_cos, f32[1024,128]{1,0:T(8,128)} %get-tuple-element.7.fine_sin), custom_call_target="tpu_custom_call" | custom-call | tf_op jit(solution)/shard_map/filter_turn/pallas_call | solution.py:225
  292.2 20.7 %correlate.1 = f32[2,16,512,512]{3,2,1,0:T(8,128)} custom-call(bf16[2,8,4,32,16,128]{5,4,3,2,1,0:T(8,128)(2,1)} %bitcast.4), custom_call_target="tpu_custom_call" | custom-call | tf_op jit(solution)/shard_map/correlate/pallas_call | solution.py:251
  (4 shorter events, 0.0 us)

commit v2 on v1

--- a/solution.py
+++ b/solution.py
@@ -13,27 +13,15 @@
 ROWS = 256
 
 
-def table_factors(chan_map, frame_len):
-    chan = jnp.repeat(chan_map, 2)
-    quarter = jnp.tile(jnp.array([0, frame_len // 4], jnp.int32), chan_map.shape[0])
-    step = 2.0 * math.pi / frame_len
-    blocks = jnp.arange(frame_len // 128, dtype=jnp.int32) * 128
-    lanes = jnp.arange(128, dtype=jnp.int32)
-    coarse = ((chan[:, None] * blocks[None, :] + quarter[:, None]) % frame_len).astype(jnp.float32) * step
-    fine = (chan[:, None] * lanes[None, :] % frame_len).astype(jnp.float32) * step
-    scale = 1.0 / math.sqrt(frame_len)
-    coarse_pair = jnp.concatenate([jnp.cos(coarse) * scale, jnp.sin(coarse) * scale], axis=1)
-    return coarse_pair, jnp.cos(fine), jnp.sin(fine)
-
-
 def turn_kernel(
-    shape, samples, gain, weights, coarse, fine_cos, fine_sin, received,
-    raw, cal, filtered, table, partial, spectra,
+    shape, samples, gain, pfb_weights, chan_map, received,
+    raw, cal, weights, filtered, table, partial, spectra,
     load_sem, halo_send, halo_recv, send_sem, recv_sem, own_sem,
 ):
     n_ta, n_ba, taps, frames, frame_len = shape
     n_dev = n_ta * n_ba
-    halo = taps - 1
+    half = CHUNK // 2
+    before, after = taps - 1 - half, half
     ta, ba = lax.axis_index("ta"), lax.axis_index("ba")
     me = ta * n_ba + ba
     table_rows = table.shape[0]
@@ -41,10 +29,17 @@
     blocks = table_rows // ROWS
     dests = n_dev // blocks
 
-    late = pltpu.make_async_copy(samples.at[pl.ds(frames - halo, halo)], raw.at[pl.ds(frames - halo, halo)], load_sem.at[0])
-    early = pltpu.make_async_copy(samples.at[pl.ds(0, frames - halo)], raw.at[pl.ds(0, frames - halo)], load_sem.at[1])
-    late.start()
-    early.start()
+    def load(index, first, count):
+        return pltpu.make_async_copy(
+            samples.at[pl.ds(first, count)], raw.at[pl.ds(first, count)], load_sem.at[index]
+        )
+
+    last = load(0, frames - before, before)
+    first = load(1, 0, after)
+    middle = load(2, after, frames - before - after)
+    last.start()
+    first.start()
+    middle.start()
 
     barrier = pltpu.get_barrier_semaphore()
 
@@ -55,40 +50,73 @@
             barrier, inc=1, device_id=(other // n_ba, lax.rem(other, n_ba)), device_id_type=MESH
         )
 
-    def calibrate(first, count):
-        pieces = frame_len // 128
+    def calibrate(start, count):
+        pieces = frame_len // 256
 
         @pl.loop(0, count * pieces)
         def _(step):
-            frame = first + step // pieces
-            rows = pl.ds(pl.multiple_of(lax.rem(step, pieces) * 128, 128), 128)
+            frame = start + step // pieces
+            rows = pl.ds(pl.multiple_of(lax.rem(step, pieces) * 256, 256), 256)
             value = raw[frame, rows, :].astype(jnp.float32) * gain[...]
-            cal[frame + halo, rows, :] = value.astype(jnp.bfloat16)
-
-    late.wait()
-    calibrate(frames - halo, halo)
-    pl.semaphore_wait(barrier, n_dev - 1)
-
-    halo_copy = pltpu.make_async_remote_copy(
-        src_ref=cal.at[pl.ds(frames, halo)],
-        dst_ref=cal.at[pl.ds(0, halo)],
-        send_sem=halo_send,
-        recv_sem=halo_recv,
+            cal[frame + before, rows, :] = value.astype(jnp.bfloat16)
+
+    forward = pltpu.make_async_remote_copy(
+        src_ref=cal.at[pl.ds(frames, before)],
+        dst_ref=cal.at[pl.ds(0, before)],
+        send_sem=halo_send.at[0],
+        recv_sem=halo_recv.at[0],
         device_id=(jnp.minimum(ta + 1, n_ta - 1), ba),
         device_id_type=MESH,
     )
+    backward = pltpu.make_async_remote_copy(
+        src_ref=cal.at[pl.ds(before, after)],
+        dst_ref=cal.at[pl.ds(before + frames, after)],
+        send_sem=halo_send.at[1],
+        recv_sem=halo_recv.at[1],
+        device_id=(lax.rem(ta + n_ta - 1, n_ta), ba),
+        device_id_type=MESH,
+    )
+
+    last.wait()
+    calibrate(frames - before, before)
+    pl.semaphore_wait(barrier, n_dev - 1)
 
     @pl.when(ta < n_ta - 1)
     def _():
-        halo_copy.start()
-
-    for a in range(frame_len // 128):
-        cos_a = coarse[:, a : a + 1]
-        sin_a = coarse[:, a + frame_len // 128 : a + frame_len // 128 + 1]
-        table[:, a * 128 : (a + 1) * 128] = (fine_cos[...] * cos_a - fine_sin[...] * sin_a).astype(jnp.bfloat16)
-
-    early.wait()
-    calibrate(0, frames - halo)
+        forward.start()
+
+    first.wait()
+    calibrate(0, after)
+    backward.start()
+    middle.wait()
+    calibrate(after, frames - before - after)
+
+    filler = jnp.zeros((128 - taps, frame_len), jnp.float32)
+    weights[...] = jnp.concatenate([pfb_weights[...], filler], axis=0).T
+
+    step_angle = 2.0 * math.pi / frame_len
+    scale = 1.0 / math.sqrt(frame_len)
+    chans = ROWS // 2
+
+    def pair(turns):
+        centred = ((turns + frame_len // 2) & (frame_len - 1)) - frame_len // 2
+        angle = centred.astype(jnp.float32) * step_angle
+        return jnp.cos(angle), jnp.sin(angle)
+
+    lane = lax.broadcasted_iota(jnp.int32, (chans, 128), 1)
+    for b in range(blocks):
+        row = chan_map[:, b * chans : (b + 1) * chans].astype(jnp.float32)
+        chan = jnp.broadcast_to(row, (128, chans)).T.astype(jnp.int32)
+        fine_cos, fine_sin = pair(chan * lane)
+        coarse_cos, coarse_sin = pair(chan * lane * 128)
+        for a in range(frame_len // 128):
+            cos_a = coarse_cos[:, a : a + 1] * scale
+            sin_a = coarse_sin[:, a : a + 1] * scale
+            columns = slice(a * 128, (a + 1) * 128)
+            real = fine_cos * cos_a - fine_sin * sin_a
+            imaginary = -(fine_sin * cos_a + fine_cos * sin_a)
+            table[b * ROWS : b * ROWS + chans, columns] = real.astype(jnp.bfloat16)
+            table[b * ROWS + chans : (b + 1) * ROWS, columns] = imaginary.astype(jnp.bfloat16)
 
     lower = 1 - ta // (n_ta // 2)
 
@@ -107,19 +135,25 @@
             spectra.at[q, pl.ds(me * rows_dev, rows_dev)], received.at[q, me], own_sem.at[q]
         )
 
-    n_chunks = frames // CHUNK
-
-    @pl.loop(0, n_chunks)
-    def _(chunk):
-        q = n_chunks - 1 - chunk
-
-        @pl.when(jnp.logical_and(chunk == n_chunks - 1, ta > 0))
+    @pl.loop(0, 2)
+    def _(q):
+        @pl.when(jnp.logical_and(q == 1, ta > 0))
         def _():
-            halo_copy.wait_recv()
-
-        @pl.when(jnp.logical_and(chunk == n_chunks - 1, ta == 0))
+            forward.wait_recv()
+
+        @pl.when(jnp.logical_and(q == 1, ta == 0))
         def _():
-            @pl.loop(0, halo)
+            @pl.loop(0, before)
+            def _(frame):
+                cal[frame] = jnp.zeros((frame_len, 128), jnp.bfloat16)
+
+        @pl.when(q == 1)
+        def _():
+            backward.wait_recv()
+
+        @pl.when(jnp.logical_and(q == 1, ta == n_ta - 1))
+        def _():
+            @pl.loop(frames + before - taps + 1, frames + before)
             def _(frame):
                 cal[frame] = jnp.zeros((frame_len, 128), jnp.bfloat16)
 
@@ -129,9 +163,11 @@
             own_weights = weights[rows, :]
             taps_here = [jnp.broadcast_to(own_weights[:, t : t + 1], (16, 128)) for t in range(taps)]
             for group in range(CHUNK // 4):
+                side = group * 4 // half
+                lead = (1 - q) * (half + side * half) + q * side * (frames - half) + group * 4 - side * half
                 sums = [None] * 4
                 for f in range(taps + 3):
-                    x = cal[q * CHUNK + group * 4 + f, rows, :].astype(jnp.float32)
+                    x = cal[lead + f, rows, :].astype(jnp.float32)
                     for j in range(4):
                         t = f - j
                         if 0 <= t < taps:
@@ -148,17 +184,19 @@
             left = table[pl.ds(base, ROWS), :]
 
             @pl.loop(0, CHUNK // 2)
-            def _(pair):
-                result = jnp.dot(left, filtered[pair], preferred_element_type=jnp.float32)
-                start = pl.multiple_of(pair * 2 * ROWS, ROWS)
+            def _(two):
+                result = jnp.dot(left, filtered[two], preferred_element_type=jnp.float32)
+                start = pl.multiple_of(two * 2 * ROWS, ROWS)
                 partial[pl.ds(start, ROWS), :] = result[:, :128]
                 partial[pl.ds(start + ROWS, ROWS), :] = result[:, 128:]
 
-            @pl.loop(0, ROWS // 8)
-            def _(k8):
+            @pl.loop(0, chans // 8)
+            def _(c8):
                 for r in range(8):
-                    k = k8 * 8 + r
-                    spectra[q, base + k] = partial[pl.ds(k, CHUNK, stride=ROWS), :].astype(jnp.bfloat16)
+                    c = c8 * 8 + r
+                    for p in range(2):
+                        values = partial[pl.ds(c + p * chans, CHUNK, stride=ROWS), :]
+                        spectra[q, base + 2 * c + p] = values.astype(jnp.bfloat16)
 
             @pl.loop(0, dests)
             def _(j):
@@ -174,9 +212,11 @@
 
     @pl.when(ta < n_ta - 1)
     def _():
-        halo_copy.wait_send()
-
-    @pl.loop(0, n_chunks)
+        forward.wait_send()
+
+    backward.wait_send()
+
+    @pl.loop(0, 2)
     def _(q):
         own(q).wait()
 
@@ -219,24 +259,24 @@
     rows_dev = table_rows // n_dev
     n_chunks = frames // CHUNK
     inputs = n_ba * samples.shape[1]
-    coarse, fine_cos, fine_sin = table_factors(chan_map, frame_len)
     vmem = pl.BlockSpec(memory_space=pltpu.VMEM)
     hbm = pl.BlockSpec(memory_space=pl.ANY)
     received = pl.pallas_call(
         functools.partial(turn_kernel, (n_ta, n_ba, taps, frames, frame_len)),
         out_shape=jax.ShapeDtypeStruct((n_chunks, n_dev, rows_dev, CHUNK, 128), jnp.bfloat16),
-        in_specs=[hbm, vmem, vmem, vmem, vmem, vmem],
+        in_specs=[hbm, vmem, vmem, vmem],
         out_specs=hbm,
         scratch_shapes=[
             pltpu.VMEM((frames, frame_len, 128), jnp.int32),
             pltpu.VMEM((frames + taps - 1, frame_len, 128), jnp.bfloat16),
+            pltpu.VMEM((frame_len, 128), jnp.float32),
             pltpu.VMEM((CHUNK // 2, frame_len, 256), jnp.bfloat16),
             pltpu.VMEM((table_rows, frame_len), jnp.bfloat16),
             pltpu.VMEM((CHUNK * ROWS, 128), jnp.float32),
             pltpu.VMEM((n_chunks, table_rows, CHUNK, 128), jnp.bfloat16),
+            pltpu.SemaphoreType.DMA((3,)),
             pltpu.SemaphoreType.DMA((2,)),
-            pltpu.SemaphoreType.DMA,
-            pltpu.SemaphoreType.DMA,
+            pltpu.SemaphoreType.DMA((2,)),
             pltpu.SemaphoreType.DMA((n_chunks, n_dev)),
             pltpu.SemaphoreType.DMA((n_chunks, n_dev)),
             pltpu.SemaphoreType.DMA((n_chunks,)),
@@ -245,7 +285,7 @@
             collective_id=0, has_side_effects=True, vmem_limit_bytes=56 * 1024 * 1024
         ),
         name="filter_turn",
-    )(samples.reshape(frames, frame_len, 128), input_gain[None, :], pfb_weights.T, coarse, fine_cos, fine_sin)
+    )(samples.reshape(frames, frame_len, 128), input_gain[None, :], pfb_weights, chan_map[None, :])
     received = received.reshape(n_chunks, n_ta, n_ba, rows_dev, CHUNK, 128)
     channels_dev = rows_dev // 2
     return pl.pallas_call(

time: 316 us -> 259 us (0.82)
  Pallas kernels: 305 us -> 259 us
  local copies, waits for them, and re-layouts: 4.05 us -> 0 us
  other arithmetic: 3.45 us -> 0 us
    pallas_call x1, Pallas kernels: 285 us -> 238 us  [per_device(): pl.pallas_call(functools.partial(turn_kernel, (n_ta, n_ba, taps, frames,...]
    sin x1 -> x0, other arithmetic: 3.22 us -> none  [table_factors(): return (coarse_pair, jnp.cos(fine), jnp.sin(fine))]
where the time goes in v2:
time: 259 us
  Pallas kernels  259 us (100%)
    pallas_call x1, Pallas kernels, per_device(): pl.pallas_call(functools.partial(turn_kernel, (n_ta, n_ba, taps, frames,...  238 us
    pallas_call x1, Pallas kernels, per_device(): pl.pallas_call(functools.partial(correlate_kernel, 1.0 / (n_ta * frames))...  20.7 us

profile of v2, /device:TPU:15, one launch (start us, length us, event | category | flops | bytes accessed | tf_op | source)
XLA Modules:
  0.0 258.5 jit_solution(3157530396338404683)
XLA Ops:
  0.0 237.8 %filter_turn.1 = bf16[2,32,32,16,128]{4,3,2,1,0:T(8,128)(2,1)} custom-call(s32[32,1024,128]{2,1,0:T(8,128)} %bitcast.5, f32[1,128]{1,0:T(1,128)} %bitcast.7, f32[16,1024]{1,0:T(8,128)} %pfb_weights.1, s32[1,512]{1,0:T(1,128)} %bitcast.6), custom_call_target="tpu_custom_call" | custom-call | tf_op jit(solution)/shard_map/filter_turn/pallas_call | solution.py:264
  237.9 20.7 %correlate.1 = f32[2,16,512,512]{3,2,1,0:T(8,128)} custom-call(bf16[2,8,4,32,16,128]{5,4,3,2,1,0:T(8,128)(2,1)} %bitcast.4), custom_call_target="tpu_custom_call" | custom-call | tf_op jit(solution)/shard_map/correlate/pallas_call | solution.py:291

commit v3 on v2

--- a/solution.py
+++ b/solution.py
@@ -27,7 +27,6 @@
     table_rows = table.shape[0]
     rows_dev = table_rows // n_dev
     blocks = table_rows // ROWS
-    dests = n_dev // blocks
 
     def load(index, first, count):
         return pltpu.make_async_copy(
@@ -118,7 +117,8 @@
             table[b * ROWS : b * ROWS + chans, columns] = real.astype(jnp.bfloat16)
             table[b * ROWS + chans : (b + 1) * ROWS, columns] = imaginary.astype(jnp.bfloat16)
 
-    lower = 1 - ta // (n_ta // 2)
+    near_base = ta // (n_ta // 2) * (n_dev // 2)
+    far_base = n_dev // 2 - near_base
 
     def message(q, dest):
         return pltpu.make_async_remote_copy(
@@ -178,8 +178,7 @@
                     filtered[s // 2, rows, (s % 2) * 128 : (s % 2 + 1) * 128] = sums[j].astype(jnp.bfloat16)
 
         @pl.loop(0, blocks)
-        def _(p):
-            b = p + (blocks - 1 - 2 * p) * lower
+        def _(b):
             base = pl.multiple_of(b * ROWS, ROWS)
             left = table[pl.ds(base, ROWS), :]
 
@@ -198,17 +197,19 @@
                         values = partial[pl.ds(c + p * chans, CHUNK, stride=ROWS), :]
                         spectra[q, base + 2 * c + p] = values.astype(jnp.bfloat16)
 
-            @pl.loop(0, dests)
-            def _(j):
-                dest = b * dests + lax.rem(j + me, dests)
-
-                @pl.when(dest != me)
-                def _():
-                    message(q, dest).start()
-
-                @pl.when(dest == me)
-                def _():
-                    own(q).start()
+        @pl.loop(0, n_dev // 2)
+        def _(j):
+            place = lax.rem(me + j, n_dev // 2)
+            message(q, far_base + place).start()
+            dest = near_base + place
+
+            @pl.when(dest != me)
+            def _():
+                message(q, dest).start()
+
+            @pl.when(dest == me)
+            def _():
+                own(q).start()
 
     @pl.when(ta < n_ta - 1)
     def _():
@@ -238,16 +239,17 @@
     n_chunks, n_ta, n_ba = received.shape[:3]
     depth = n_chunks * n_ta * received.shape[4]
 
-    def part(p):
+    def part(row):
         return jnp.concatenate(
-            [received[:, :, b, p].reshape(depth, 128) for b in range(n_ba)], axis=1
-        )
-
-    re, im = part(0), part(1)
-    right = jnp.concatenate([re, im], axis=0)
-    re_t, im_t = re.T, im.T
-    out[0, 0] = jnp.dot(jnp.concatenate([re_t, im_t], axis=1), right, preferred_element_type=jnp.float32) * scale
-    out[1, 0] = jnp.dot(jnp.concatenate([im_t, -re_t], axis=1), right, preferred_element_type=jnp.float32) * scale
+            [received[:, :, b, row].reshape(depth, 128) for b in range(n_ba)], axis=1
+        )
+
+    for c in range(out.shape[1]):
+        re, im = part(2 * c), part(2 * c + 1)
+        right = jnp.concatenate([re, im], axis=0)
+        re_t, im_t = re.T, im.T
+        out[0, c] = jnp.dot(jnp.concatenate([re_t, im_t], axis=1), right, preferred_element_type=jnp.float32) * scale
+        out[1, c] = jnp.dot(jnp.concatenate([im_t, -re_t], axis=1), right, preferred_element_type=jnp.float32) * scale
 
 
 def per_device(samples, input_gain, pfb_weights, chan_map):
@@ -290,10 +292,10 @@
     channels_dev = rows_dev // 2
     return pl.pallas_call(
         functools.partial(correlate_kernel, 1.0 / (n_ta * frames)),
-        grid=(channels_dev,),
+        grid=(channels_dev // 2,),
         out_shape=jax.ShapeDtypeStruct((2, channels_dev, inputs, inputs), jnp.float32),
-        in_specs=[pl.BlockSpec((n_chunks, n_ta, n_ba, 2, CHUNK, 128), lambda c: (0, 0, 0, c, 0, 0))],
-        out_specs=pl.BlockSpec((2, 1, inputs, inputs), lambda c: (0, c, 0, 0)),
+        in_specs=[pl.BlockSpec((n_chunks, n_ta, n_ba, 4, CHUNK, 128), lambda c: (0, 0, 0, c, 0, 0))],
+        out_specs=pl.BlockSpec((2, 2, inputs, inputs), lambda c: (0, c, 0, 0)),
         compiler_params=pltpu.CompilerParams(vmem_limit_bytes=48 * 1024 * 1024),
         name="correlate",
     )(received)

time: 259 us -> 263 us (1.015)
    pallas_call x1, Pallas kernels: 238 us -> 243 us  [per_device(): pl.pallas_call(functools.partial(turn_kernel, (n_ta, n_ba, taps, frames,...]
    pallas_call x1, Pallas kernels: 20.7 us -> 16.7 us  [per_device(): pl.pallas_call(functools.partial(correlate_kernel, 1.0 / (n_ta * frames))...]
where the time goes in v3:
time: 263 us; the launch traced here: 260 us
  Pallas kernels  260 us (99%)
    pallas_call x1, Pallas kernels, per_device(): pl.pallas_call(functools.partial(turn_kernel, (n_ta, n_ba, taps, frames,...  243 us
    pallas_call x1, Pallas kernels, per_device(): pl.pallas_call(functools.partial(correlate_kernel, 1.0 / (n_ta * frames))...  16.7 us

profile of v3, /device:TPU:15, one launch (start us, length us, event | category | flops | bytes accessed | tf_op | source)
XLA Modules:
  0.0 260.2 jit_solution(14906222106161257374)
XLA Ops:
  0.0 243.5 %filter_turn.1 = bf16[2,32,32,16,128]{4,3,2,1,0:T(8,128)(2,1)} custom-call(s32[32,1024,128]{2,1,0:T(8,128)} %bitcast.5, f32[1,128]{1,0:T(1,128)} %bitcast.7, f32[16,1024]{1,0:T(8,128)} %pfb_weights.1, s32[1,512]{1,0:T(1,128)} %bitcast.6), custom_call_target="tpu_custom_call" | custom-call | tf_op jit(solution)/shard_map/filter_turn/pallas_call | solution.py:266
  243.5 16.7 %correlate.1 = f32[2,16,512,512]{3,2,1,0:T(8,128)} custom-call(bf16[2,8,4,32,16,128]{5,4,3,2,1,0:T(8,128)(2,1)} %bitcast.4), custom_call_target="tpu_custom_call" | custom-call | tf_op jit(solution)/shard_map/correlate/pallas_call | solution.py:293

commit v4 on v3

--- a/solution.py
+++ b/solution.py
@@ -137,19 +137,11 @@
 
     @pl.loop(0, 2)
     def _(q):
-        @pl.when(jnp.logical_and(q == 1, ta > 0))
-        def _():
-            forward.wait_recv()
-
         @pl.when(jnp.logical_and(q == 1, ta == 0))
         def _():
             @pl.loop(0, before)
             def _(frame):
                 cal[frame] = jnp.zeros((frame_len, 128), jnp.bfloat16)
-
-        @pl.when(q == 1)
-        def _():
-            backward.wait_recv()
 
         @pl.when(jnp.logical_and(q == 1, ta == n_ta - 1))
         def _():
@@ -197,19 +189,32 @@
                         values = partial[pl.ds(c + p * chans, CHUNK, stride=ROWS), :]
                         spectra[q, base + 2 * c + p] = values.astype(jnp.bfloat16)
 
+        @pl.when(jnp.logical_and(q == 0, ta > 0))
+        def _():
+            forward.wait_recv()
+
+        @pl.when(q == 0)
+        def _():
+            backward.wait_recv()
+
         @pl.loop(0, n_dev // 2)
         def _(j):
             place = lax.rem(me + j, n_dev // 2)
             message(q, far_base + place).start()
-            dest = near_base + place
-
-            @pl.when(dest != me)
+
+            @pl.when(q == 1)
             def _():
-                message(q, dest).start()
-
-            @pl.when(dest == me)
-            def _():
-                own(q).start()
+                dest = near_base + place
+
+                @pl.when(dest != me)
+                def _():
+                    message(0, dest).start()
+                    message(1, dest).start()
+
+                @pl.when(dest == me)
+                def _():
+                    own(0).start()
+                    own(1).start()
 
     @pl.when(ta < n_ta - 1)
     def _():

time: 263 us -> 311 us (1.18)
  the two profiles are of different devices: /device:TPU:15 before, /device:TPU:3 now
where the time goes in v4:
time: 311 us; the launch traced here: 310 us
  Pallas kernels  310 us (100%)
    pallas_call x1, Pallas kernels, per_device(): pl.pallas_call(functools.partial(turn_kernel, (n_ta, n_ba, taps, frames,...  293 us
    pallas_call x1, Pallas kernels, per_device(): pl.pallas_call(functools.partial(correlate_kernel, 1.0 / (n_ta * frames))...  16.7 us

profile of v4, /device:TPU:3, one launch (start us, length us, event | category | flops | bytes accessed | tf_op | source)
XLA Modules:
  0.0 310.1 jit_solution(12747733532660345189)
XLA Ops:
  0.0 293.4 %filter_turn.1 = bf16[2,32,32,16,128]{4,3,2,1,0:T(8,128)(2,1)} custom-call(s32[32,1024,128]{2,1,0:T(8,128)} %bitcast.5, f32[1,128]{1,0:T(1,128)} %bitcast.7, f32[16,1024]{1,0:T(8,128)} %pfb_weights.1, s32[1,512]{1,0:T(1,128)} %bitcast.6), custom_call_target="tpu_custom_call" | custom-call | tf_op jit(solution)/shard_map/filter_turn/pallas_call | solution.py:271
  293.4 16.7 %correlate.1 = f32[2,16,512,512]{3,2,1,0:T(8,128)} custom-call(bf16[2,8,4,32,16,128]{5,4,3,2,1,0:T(8,128)(2,1)} %bitcast.4), custom_call_target="tpu_custom_call" | custom-call | tf_op jit(solution)/shard_map/correlate/pallas_call | solution.py:298

commit v5 on v2

--- a/solution.py
+++ b/solution.py
@@ -60,22 +60,27 @@
             value = raw[frame, rows, :].astype(jnp.float32) * gain[...]
             cal[frame + before, rows, :] = value.astype(jnp.bfloat16)
 
-    forward = pltpu.make_async_remote_copy(
-        src_ref=cal.at[pl.ds(frames, before)],
-        dst_ref=cal.at[pl.ds(0, before)],
-        send_sem=halo_send.at[0],
-        recv_sem=halo_recv.at[0],
-        device_id=(jnp.minimum(ta + 1, n_ta - 1), ba),
-        device_id_type=MESH,
-    )
-    backward = pltpu.make_async_remote_copy(
-        src_ref=cal.at[pl.ds(before, after)],
-        dst_ref=cal.at[pl.ds(before + frames, after)],
-        send_sem=halo_send.at[1],
-        recv_sem=halo_recv.at[1],
-        device_id=(lax.rem(ta + n_ta - 1, n_ta), ba),
-        device_id_type=MESH,
-    )
+    def halo_copy(index, source, target, count, shard):
+        return pltpu.make_async_remote_copy(
+            src_ref=cal.at[pl.ds(source, count)],
+            dst_ref=cal.at[pl.ds(target, count)],
+            send_sem=halo_send.at[index],
+            recv_sem=halo_recv.at[index],
+            device_id=(shard, ba),
+            device_id_type=MESH,
+        )
+
+    after_me = jnp.minimum(ta + 1, n_ta - 1)
+    before_me = lax.rem(ta + n_ta - 1, n_ta)
+    cut = half // 2
+    forward = [
+        halo_copy(0, frames, 0, cut, after_me),
+        halo_copy(1, frames + cut, cut, before - cut, after_me),
+    ]
+    backward = [
+        halo_copy(2, before, before + frames, cut, before_me),
+        halo_copy(3, before + cut, before + frames + cut, after - cut, before_me),
+    ]
 
     last.wait()
     calibrate(frames - before, before)
@@ -83,11 +88,13 @@
 
     @pl.when(ta < n_ta - 1)
     def _():
-        forward.start()
+        for copy in forward:
+            copy.start()
 
     first.wait()
     calibrate(0, after)
-    backward.start()
+    for copy in backward:
+        copy.start()
     middle.wait()
     calibrate(after, frames - before - after)
 
@@ -139,7 +146,8 @@
     def _(q):
         @pl.when(jnp.logical_and(q == 1, ta > 0))
         def _():
-            forward.wait_recv()
+            for copy in forward:
+                copy.wait_recv()
 
         @pl.when(jnp.logical_and(q == 1, ta == 0))
         def _():
@@ -149,7 +157,8 @@
 
         @pl.when(q == 1)
         def _():
-            backward.wait_recv()
+            for copy in backward:
+                copy.wait_recv()
 
         @pl.when(jnp.logical_and(q == 1, ta == n_ta - 1))
         def _():
@@ -212,9 +221,11 @@
 
     @pl.when(ta < n_ta - 1)
     def _():
-        forward.wait_send()
-
-    backward.wait_send()
+        for copy in forward:
+            copy.wait_send()
+
+    for copy in backward:
+        copy.wait_send()
 
     @pl.loop(0, 2)
     def _(q):
@@ -238,16 +249,17 @@
     n_chunks, n_ta, n_ba = received.shape[:3]
     depth = n_chunks * n_ta * received.shape[4]
 
-    def part(p):
+    def part(row):
         return jnp.concatenate(
-            [received[:, :, b, p].reshape(depth, 128) for b in range(n_ba)], axis=1
-        )
-
-    re, im = part(0), part(1)
-    right = jnp.concatenate([re, im], axis=0)
-    re_t, im_t = re.T, im.T
-    out[0, 0] = jnp.dot(jnp.concatenate([re_t, im_t], axis=1), right, preferred_element_type=jnp.float32) * scale
-    out[1, 0] = jnp.dot(jnp.concatenate([im_t, -re_t], axis=1), right, preferred_element_type=jnp.float32) * scale
+            [received[:, :, b, row].reshape(depth, 128) for b in range(n_ba)], axis=1
+        )
+
+    for c in range(out.shape[1]):
+        re, im = part(2 * c), part(2 * c + 1)
+        right = jnp.concatenate([re, im], axis=0)
+        re_t, im_t = re.T, im.T
+        out[0, c] = jnp.dot(jnp.concatenate([re_t, im_t], axis=1), right, preferred_element_type=jnp.float32) * scale
+        out[1, c] = jnp.dot(jnp.concatenate([im_t, -re_t], axis=1), right, preferred_element_type=jnp.float32) * scale
 
 
 def per_device(samples, input_gain, pfb_weights, chan_map):
@@ -275,8 +287,8 @@
             pltpu.VMEM((CHUNK * ROWS, 128), jnp.float32),
             pltpu.VMEM((n_chunks, table_rows, CHUNK, 128), jnp.bfloat16),
             pltpu.SemaphoreType.DMA((3,)),
-            pltpu.SemaphoreType.DMA((2,)),
-            pltpu.SemaphoreType.DMA((2,)),
+            pltpu.SemaphoreType.DMA((4,)),
+            pltpu.SemaphoreType.DMA((4,)),
             pltpu.SemaphoreType.DMA((n_chunks, n_dev)),
             pltpu.SemaphoreType.DMA((n_chunks, n_dev)),
             pltpu.SemaphoreType.DMA((n_chunks,)),
@@ -290,10 +302,10 @@
     channels_dev = rows_dev // 2
     return pl.pallas_call(
         functools.partial(correlate_kernel, 1.0 / (n_ta * frames)),
-        grid=(channels_dev,),
+        grid=(channels_dev // 2,),
         out_shape=jax.ShapeDtypeStruct((2, channels_dev, inputs, inputs), jnp.float32),
-        in_specs=[pl.BlockSpec((n_chunks, n_ta, n_ba, 2, CHUNK, 128), lambda c: (0, 0, 0, c, 0, 0))],
-        out_specs=pl.BlockSpec((2, 1, inputs, inputs), lambda c: (0, c, 0, 0)),
+        in_specs=[pl.BlockSpec((n_chunks, n_ta, n_ba, 4, CHUNK, 128), lambda c: (0, 0, 0, c, 0, 0))],
+        out_specs=pl.BlockSpec((2, 2, inputs, inputs), lambda c: (0, c, 0, 0)),
         compiler_params=pltpu.CompilerParams(vmem_limit_bytes=48 * 1024 * 1024),
         name="correlate",
     )(received)

time: 259 us -> 255 us (0.985)
  Pallas kernels: 259 us -> 255 us
    pallas_call x1, Pallas kernels: 20.7 us -> 16.7 us  [per_device(): pl.pallas_call(functools.partial(correlate_kernel, 1.0 / (n_ta * frames))...]
where the time goes in v5:
time: 255 us
  Pallas kernels  255 us (100%)
    pallas_call x1, Pallas kernels, per_device(): pl.pallas_call(functools.partial(turn_kernel, (n_ta, n_ba, taps, frames,...  238 us
    pallas_call x1, Pallas kernels, per_device(): pl.pallas_call(functools.partial(correlate_kernel, 1.0 / (n_ta * frames))...  16.7 us

profile of v5, /device:TPU:15, one launch (start us, length us, event | category | flops | bytes accessed | tf_op | source)
XLA Modules:
  0.0 254.6 jit_solution(17104626994493009922)
XLA Ops:
  0.0 237.9 %filter_turn.1 = bf16[2,32,32,16,128]{4,3,2,1,0:T(8,128)(2,1)} custom-call(s32[32,1024,128]{2,1,0:T(8,128)} %bitcast.5, f32[1,128]{1,0:T(1,128)} %bitcast.7, f32[16,1024]{1,0:T(8,128)} %pfb_weights.1, s32[1,512]{1,0:T(1,128)} %bitcast.6), custom_call_target="tpu_custom_call" | custom-call | tf_op jit(solution)/shard_map/filter_turn/pallas_call | solution.py:276
  237.9 16.7 %correlate.1 = f32[2,16,512,512]{3,2,1,0:T(8,128)} custom-call(bf16[2,8,4,32,16,128]{5,4,3,2,1,0:T(8,128)(2,1)} %bitcast.4), custom_call_target="tpu_custom_call" | custom-call | tf_op jit(solution)/shard_map/correlate/pallas_call | solution.py:303
